TPU v7x, 512 devices: a whole 4x4x16 slice. The times are simulated.
512 devices in a mesh: sgroup: 32 (over z_lo, y), tile: 16 (over x, z_hi, core).
Axes of the slice: x: 4, y: 4, z: 16 (z_hi: 2, z_lo: 8; z = z_hi * 8 + z_lo), core: 2. Of those that a mesh axis runs over, the one named last changes fastest.
Arguments:
- voltages: bfloat16 [2, 512, 256, 2, 16, 128], P(None, 'sgroup', 'tile'), may hold values from -6 to 6
- weights: bfloat16 [2, 512, 256, 2, 16], P(None, 'sgroup'), may hold values from -0.25 to 0.25
- antenna_slot_index: int32 [512, 256], P('sgroup', 'tile'), may hold values from 0 to 255, each once within a row
- station_order: int32 [512], replicated, may hold values from 0 to 511, each once
Outputs:
- visibilities: float32 [16, 2, 1024, 1024], P('tile', None, 'sgroup')
Inputs may be any that keep to these rules, and one draw needn't show every extreme that they name: `station_order`: each station slot holds a different station. `antenna_slot_index`: within each station slot, each antenna slot holds a different antenna.
All inputs are finite; a program needn't handle non-finite values.
Results may differ from a plain program's by a relative error of at most 0.0038.
Values may be sent and summed in bfloat16 or wider, within the bound.
A program may use at most 64 MiB of HBM per device.

v0:
```python
import jax
import jax.numpy as jnp
from jax import lax
from jax.sharding import PartitionSpec as P


def in_blocks(array, dim, size):
    dims = array.shape
    pieces = array.reshape(*dims[:dim], size, dims[dim] // size, *dims[dim + 1 :])
    return jnp.moveaxis(pieces, dim, 0)


def sent_and_summed(array, axis, dim):
    size = lax.axis_size(axis)
    pieces = lax.all_to_all(in_blocks(array, dim, size), axis, 0, 0, tiled=True)
    return jnp.sum(pieces, axis=0)


def in_order(pieces, dim):
    pieces = jnp.moveaxis(pieces, 0, dim)
    dims = pieces.shape
    return pieces.reshape(*dims[:dim], dims[dim] * dims[dim + 1], *dims[dim + 2 :])


def from_everyone(array, axis):
    copies = jnp.broadcast_to(array, (lax.axis_size(axis), *array.shape))
    return lax.all_to_all(copies, axis, split_axis=0, concat_axis=0, tiled=True)


def collect(array, axis, dim):
    return in_order(from_everyone(array, axis), dim)


def mix(left, right):
    return jnp.einsum("sapc,sapct->cspt", left, right, preferred_element_type=jnp.float32)


def cross(left, right, form):
    return jnp.einsum(form, left, right, preferred_element_type=jnp.float32)


def body(voltages, weights, antenna_slot_index, station_order):
    st_local = voltages.shape[1]
    slots = jnp.arange(st_local, dtype=jnp.int32)[:, None]
    chosen = weights[:, slots, antenna_slot_index]
    real_beam = mix(chosen[0], voltages[0]) - mix(chosen[1], voltages[1])
    imag_beam = mix(chosen[0], voltages[1]) + mix(chosen[1], voltages[0])
    partial_value = jnp.stack([real_beam, imag_beam], axis=1)
    summed = sent_and_summed(partial_value, "tile", 0)
    beams = summed.astype(jnp.bfloat16)
    gathered = collect(beams, "sgroup", 2)
    placed = jnp.zeros_like(gathered).at[:, :, station_order].set(gathered)
    ch_local, _, stations, polars, spectra = placed.shape
    every_row = placed.reshape(ch_local, 2, stations * polars, spectra)
    block = st_local * polars
    group = lax.axis_index("sgroup")
    local_station_rows = lax.dynamic_slice_in_dim(every_row, group * block, block, 2)
    scale = 1.0 / spectra
    visibility_real = cross(local_station_rows[:, 0], every_row[:, 0], "crt,cjt->crj") + cross(
        local_station_rows[:, 1], every_row[:, 1], "crt,cjt->crj"
    )
    imag_vis = cross(local_station_rows[:, 1], every_row[:, 0], "crt,cjt->crj") - cross(
        local_station_rows[:, 0], every_row[:, 1], "crt,cjt->crj"
    )
    return jnp.stack([visibility_real * scale, imag_vis * scale], axis=1)


def solution(mesh):
    in_specs = (
        P(None, "sgroup", "tile", None, None, None),
        P(None, "sgroup", None, None, None),
        P("sgroup", "tile"),
        P(),
    )
    out_specs = P("tile", None, "sgroup", None)
    return jax.shard_map(body, mesh=mesh, in_specs=in_specs, out_specs=out_specs, check_vma=False)
```

profile of v0, /device:TPU:1, one launch (start us, length us, event | category | flops | bytes accessed | tf_op | source)
XLA Modules:
  0.0 139.1 jit_solution(646553634424828144)
XLA Ops:
  0.0 9.8 %copy.7 = bf16[2,16,256,2,16]{4,3,2,1,0:T(2,128)(2,1)} copy(bf16[2,16,256,2,16]{2,4,3,1,0:T(8,128)(2,1)} %param.5) | data formatting | bytes 1048576 | tf_op args[1]
  9.9 3.7 %gather_fusion = bf16[256,2,2,16]{3,2,1,0:T(2,128)(2,1)S(1)} fusion(bf16[2,16,256,2,16]{4,3,2,1,0:T(2,128)(2,1)} %copy.7, s32[256]{0:T(256)S(1)} %reshape.58), kind=kCustom, calls=%fused_computation | custom fusion | bytes 67584 | tf_op jit(solution)/shard_map/gather | solution.py:45
  13.6 0.2 slice_bitcast_fusion.8
  13.8 0.5 copy.12
  14.2 4.5 %slice_bitcast_fusion.1 = (bf16[16,16,2,16,128]{4,3,2,1,0:T(8,128)(2,1)S(1)}, bf16[16,16,2,16,128]{4,3,2,1,0:T(8,128)(2,1)}) fusion(bf16[2,16,16,2,16,128]{5,4,3,2,1,0:T(8,128)(2,1)} %param.4), kind=kLoop, calls=%fused_computation.3 | loop fusion | bytes 8388608 | tf_op jit(solution)/shard_map/squeeze | solution.py:46
  18.7 0.5 copy.9
  19.2 3.2 %fusion.2 = f32[16,16,2,1,128]{4,3,2,1,0:T(1,128)S(1)} fusion(bf16[16,16,2,16,1]{1,4,2,0,3:T(2,128)(2,1)S(1)} %copy.12, bf16[16,16,2,16,128]{4,3,2,1,0:T(8,128)(2,1)} %get-tuple-element.6), kind=kOutput, calls=%fused_computation.6 | convolution fusion | flops 2097152 | bytes 2375680 | tf_op jit(solution)/shard_map/sapc,sapct->cspt/dot_general | solution.py:35
  22.4 1.5 %fusion = f32[16,16,2,1,128]{4,3,2,1,0:T(1,128)S(1)} fusion(bf16[16,16,2,16,1]{1,4,2,0,3:T(2,128)(2,1)S(1)} %copy.9, bf16[16,16,2,16,128]{4,3,2,1,0:T(8,128)(2,1)S(1)} %copy-done), kind=kOutput, calls=%fused_computation.4 | convolution fusion | flops 2097152 | bytes 2375680 | tf_op jit(solution)/shard_map/sapc,sapct->cspt/dot_general | solution.py:35
  23.9 1.4 %fusion.4 = f32[16,16,2,1,128]{4,3,2,1,0:T(1,128)S(1)} fusion(bf16[16,16,2,16,1]{1,4,2,0,3:T(2,128)(2,1)S(1)} %copy.12, bf16[16,16,2,16,128]{4,3,2,1,0:T(8,128)(2,1)S(1)} %get-tuple-element.5), kind=kOutput, calls=%fused_computation.8 | convolution fusion | flops 2097152 | bytes 2375680 | tf_op jit(solution)/shard_map/sapc,sapct->cspt/dot_general | solution.py:35
  25.3 1.4 %fusion.6 = f32[16,16,2,1,128]{4,3,2,1,0:T(1,128)S(1)} fusion(bf16[16,16,2,16,1]{1,4,2,0,3:T(2,128)(2,1)S(1)} %copy.9, bf16[16,16,2,16,128]{4,3,2,1,0:T(8,128)(2,1)S(1)} %get-tuple-element.5), kind=kOutput, calls=%fused_computation.10 | convolution fusion | flops 2097152 | bytes 2375680 | tf_op jit(solution)/shard_map/sapc,sapct->cspt/dot_general | solution.py:35
  26.7 0.3 add_bitcast_fusion
  27.1 0.3 maximum_bitcast_fusion
  27.4 38.2 %all_to_all.10 = f32[16,1,2,16,2,128]{5,4,3,2,1,0:T(2,128)S(1)} all-to-all(f32[16,1,2,16,2,128]{5,4,3,2,1,0:T(2,128)S(1)} %maximum_bitcast_fusion), channel_id=1, replica_groups=mesh['sgroup'=32,'tile'=16] {'tile'}, dimensions={0} | all-to-all | bytes 1048576 | tf_op jit(solution)/shard_map/all_to_all | solution.py:15
  65.6 0.2 reduce_sum.9
  65.8 1.3 broadcast_in_dim.22
  67.0 23.3 %all-to-all-start.1 = ((bf16[32,1,2,16,2,128]{5,4,2,3,1,0:T(2,128)(2,1)}), bf16[32,1,2,16,2,128]{5,4,2,3,1,0:T(2,128)(2,1)S(1)}, u32[]{:S(2)}, u32[]{:S(2)}) async-start(bf16[32,1,2,16,2,128]{5,4,2,3,1,0:T(2,128)(2,1)} %broadcast_in_dim.22), calls=%async_computation.1 | async-start | bytes 1048576 | tf_op jit(solution)/shard_map/all_to_all | solution.py:27
  90.4 26.7 %all-to-all-done.1 = bf16[32,1,2,16,2,128]{5,4,2,3,1,0:T(2,128)(2,1)S(1)} async-done(((bf16[32,1,2,16,2,128]{5,4,2,3,1,0:T(2,128)(2,1)}), bf16[32,1,2,16,2,128]{5,4,2,3,1,0:T(2,128)(2,1)S(1)}, u32[]{:S(2)}, u32[]{:S(2)}) %all-to-all-start.1) | async-done | bytes 524320 | tf_op jit(solution)/shard_map/all_to_all | solution.py:27
  117.1 0.3 broadcast.24
  117.4 20.2 %scatter_fusion = bf16[2,512,2,128]{3,2,1,0:T(2,128)(2,1)S(1)} fusion(bf16[2,512,2,128]{3,2,1,0:T(2,128)(2,1)S(1)} %broadcast.24, s32[512]{0:T(512)S(1)} %compare_select_fusion.1, bf16[512,2,2,128]{3,2,1,0:T(2,128)(2,1)S(1)} %bitcast.67), kind=kCustom, calls=%fused_computation.1 | custom fusion | bytes 1574912 | tf_op jit(solution)/shard_map/scatter | solution.py:52
  137.6 0.2 fusion.13
  137.8 0.2 fusion.12
  138.0 0.2 fusion.11
  138.2 0.2 fusion.9
  138.4 0.7 pad_maximum_fusion
  (10 shorter events, 0.1 us)
Async XLA Ops:
  0.0 9.8 %copy-start.1 = (s32[16,16]{1,0:T(8,128)S(1)}, s32[16,16]{1,0:T(8,128)}, u32[]{:S(2)}) copy-start(s32[16,16]{1,0:T(8,128)} %param.6) | copy-start | bytes 3076
  19.2 3.2 %copy-start = (bf16[16,16,2,16,128]{4,3,2,1,0:T(8,128)(2,1)S(1)}, bf16[16,16,2,16,128]{4,3,2,1,0:T(8,128)(2,1)}, u32[]{:S(2)}) copy-start(bf16[16,16,2,16,128]{4,3,2,1,0:T(8,128)(2,1)} %get-tuple-element.6) | copy-start | bytes 6291460
  27.0 63.3 %copy-start.2 = (s32[512]{0:T(512)S(1)}, s32[512]{0:T(512)}, u32[]{:S(2)}) copy-start(s32[512]{0:T(512)} %param.7) | copy-start | bytes 6148
  67.0 50.0 %all-to-all-start.1 = ((bf16[32,1,2,16,2,128]{5,4,2,3,1,0:T(2,128)(2,1)}), bf16[32,1,2,16,2,128]{5,4,2,3,1,0:T(2,128)(2,1)S(1)}, u32[]{:S(2)}, u32[]{:S(2)}) async-start(bf16[32,1,2,16,2,128]{5,4,2,3,1,0:T(2,128)(2,1)} %broadcast_in_dim.22), calls=%async_computation.1 | async-start | bytes 1048576 | tf_op jit(solution)/shard_map/all_to_all | solution.py:27
where the time goes:
time: 142 us; the launch traced here: 139 us
  local copies, waits for them, and re-layouts  41 us (29%)
  blocking collectives  38.2 us (27%)
  waiting for transfers between devices  26.7 us (19%)
  starting transfers between devices  23.3 us (16%)
  matrix products  8.27 us (6%)
  other arithmetic  1.51 us (1%)
    all_to_all x1, blocking collectives, sent_and_summed(): pieces = lax.all_to_all(in_blocks(array, dim, size), axis, 0, 0, tiled=True)  38.2 us
    all_to_all x1, waiting for transfers between devices, from_everyone(): return lax.all_to_all(copies, axis, split_axis=0, concat_axis=0, tiled=True)  26.7 us
    all_to_all x1, starting transfers between devices, from_everyone(): return lax.all_to_all(copies, axis, split_axis=0, concat_axis=0, tiled=True)  23.3 us
    scatter x1, local copies, waits for them, and re-layouts, body(): placed = jnp.zeros_like(gathered).at[:, :, station_order].set(gathered)  20.2 us
    unnamed x7, local copies, waits for them, and re-layouts  9.77 us
    dot_general x4, matrix products, mix(): jnp.einsum('sapc,sapct->cspt', left, right, preferred_element_type=jnp.fl...  7.52 us
    squeeze x4, local copies, waits for them, and re-layouts, body(): real_beam = mix(chosen[0], voltages[0]) - mix(chosen[1], voltages[1])  5.63 us
    gather x1, local copies, waits for them, and re-layouts, body(): chosen = weights[:, slots, antenna_slot_index]  3.69 us
  transfers between devices with their start and end apart: 1, of which 1 were waited for; matrix products, arithmetic and copies ran while one was open for 0% of the time, Pallas kernels for 0%

commit v1 on v0

v1 whole, which is shorter than its diff:
```python
import functools

import jax
import jax.numpy as jnp
from jax import lax
from jax.experimental import pallas as pl
from jax.experimental.pallas import tpu as pltpu
from jax.sharding import PartitionSpec as P

MESH = pl.DeviceIdType.MESH
F32, BF16, I32 = jnp.float32, jnp.bfloat16, jnp.int32
X_TYPE, Z_TYPE = BF16, F32
STATIONS, SLOTS, POLARS, CHANNELS, SPECTRA, ANTENNAS = 16, 16, 2, 16, 128, 256


def iota(shape, dim):
    return lax.broadcasted_iota(I32, shape, dim)


def as_bf16(mask):
    return jnp.where(mask, 1.0, 0.0).astype(BF16)


def kernel(
    volt, wt, idx_in, order_in, out,
    idx, order, vbuf, wbuf, wexp, part, core_in, x_out, x_in, z_own, z_out, z_in, held, perm, ordered,
    i_sem, v_sem, w_sem, core_s, core_r, x_s, x_r, zi_s, zi_r, z1_s, z1_r, z2_s, z2_r, y_s, y_r, f_s, f_r,
):
    group, tile = lax.axis_index("sgroup"), lax.axis_index("tile")
    zh4, zq, y = group // 16, (group // 4) % 4, group % 4
    x, zi, core = tile // 4, (tile // 2) % 2, tile % 2

    def at(g, t):
        return {"sgroup": g, "tile": t}

    sibling = at(group, x * 4 + zi * 2 + (1 - core))
    x_peer = [at(group, ((x + d) % 4) * 4 + zi * 2 + core) for d in (1, 2, 3)]
    zi_peer = at(group, x * 4 + (1 - zi) * 2 + core)
    z1_peer = at((1 - zh4) * 16 + zq * 4 + y, tile)
    z2_peer = [at(zh4 * 16 + ((zq + d) % 4) * 4 + y, tile) for d in (1, 2, 3)]
    y_next, y_last = (y + 1) % 4, (y + 3) % 4
    y_peer = [at(zh4 * 16 + zq * 4 + y_next, tile), at(zh4 * 16 + zq * 4 + y_last, tile)]

    barrier = pltpu.get_barrier_semaphore()
    partners = [sibling, *x_peer, zi_peer, z1_peer, *z2_peer, *y_peer]

    small = [
        pltpu.make_async_copy(idx_in, idx, i_sem.at[0]),
        pltpu.make_async_copy(order_in, order, i_sem.at[1]),
    ]
    for copy in small:
        copy.start()
    w_copy = pltpu.make_async_copy(wt, wbuf, w_sem)
    w_copy.start()
    v_copies = []
    for p in range(POLARS):
        for q in range(2):
            copy = pltpu.make_async_copy(
                volt.at[:, pl.ds(q * 8, 8), :, p], vbuf.at[p, :, pl.ds(q * 8, 8)], v_sem.at[p, q]
            )
            copy.start()
            v_copies.append(copy)

    for partner in partners:
        pl.semaphore_signal(barrier, inc=1, device_id=partner, device_id_type=MESH)
    pl.semaphore_wait(barrier, len(partners))

    started = []

    def send(src, dst, s, r, device):
        copy = pltpu.make_async_remote_copy(
            src_ref=src, dst_ref=dst, send_sem=s, recv_sem=r, device_id=device, device_id_type=MESH
        )
        copy.start()
        started.append(copy)

    def arrived(dst, s, r):
        pltpu.make_async_remote_copy(
            src_ref=dst, dst_ref=dst, send_sem=s, recv_sem=r, device_id=sibling, device_id_type=MESH
        ).wait_recv()

    for copy in small:
        copy.wait()
    lanes = SLOTS * CHANNELS
    spread = as_bf16(iota((SLOTS, lanes), 0) == iota((SLOTS, lanes), 1) % SLOTS)
    wide = jnp.dot(idx[...].astype(BF16), spread, preferred_element_type=F32)
    own_lane = iota((STATIONS, lanes), 0) == iota((STATIONS, lanes), 1) // SLOTS
    wide = jnp.where(own_lane, wide, 0.0).astype(BF16)
    number = jnp.dot(jnp.ones((ANTENNAS, STATIONS), BF16), wide, preferred_element_type=F32)
    onehot = as_bf16(number == iota((ANTENNAS, lanes), 0).astype(F32))
    unfold = as_bf16(iota((lanes, lanes), 0) % SLOTS == iota((lanes, lanes), 1) // CHANNELS)
    w_copy.wait()

    def pick(step, carry):
        kept = (step % 2) * 8 + iota((256, lanes), 0) // 32 == iota((256, lanes), 1) // SLOTS
        block = wbuf[pl.ds(pl.multiple_of(step * 256, 256), 256), :]
        got = jnp.dot(block, onehot, preferred_element_type=F32)
        got = jnp.where(kept, got, 0.0).astype(BF16)
        got = jnp.dot(got, unfold, preferred_element_type=F32)
        same = iota((256, lanes), 0) % CHANNELS == iota((256, lanes), 1) % CHANNELS
        wexp[pl.ds(pl.multiple_of(step * 256, 256), 256), :] = jnp.where(same, got, 0.0).astype(BF16)
        return carry

    lax.fori_loop(0, 4, pick, 0)

    slabs = part.reshape(POLARS, 4, 2, 2, 2, STATIONS, SPECTRA)
    for p in range(POLARS):
        for q in range(2):
            v_copies[p * 2 + q].wait()
            for s in range(q * 8, q * 8 + 8):
                left = jnp.concatenate(
                    [wexp[pl.ds(((k * STATIONS + s) * 2 + p) * 16, 16), :] for k in (0, 1)], axis=0
                )
                right = jnp.concatenate(
                    [vbuf[p, k, s].reshape(lanes, SPECTRA) for k in (0, 1)], axis=1
                )
                both = jnp.dot(left, right, preferred_element_type=F32)
                real = both[:16, :SPECTRA] - both[16:, SPECTRA:]
                imag = both[:16, SPECTRA:] + both[16:, :SPECTRA]
                part[pl.ds(p * 512 + s, 16, stride=32), :] = real
                part[pl.ds(p * 512 + 16 + s, 16, stride=32), :] = imag
        send(slabs.at[p, :, :, 1 - core], core_in.at[p], core_s.at[p], core_r.at[p], sibling)

    lane_row = jnp.concatenate([order[...] * 2, order[...] * 2 + 1], axis=1)

    def fill(step, carry):
        rows = step * 64 + iota((64, 1024), 0)
        perm[pl.ds(pl.multiple_of(step * 64, 64), 64), :] = as_bf16(rows == lane_row)
        return carry

    lax.fori_loop(0, 4, fill, 0)
    for p in range(POLARS):
        arrived(core_in.at[p], core_s.at[p], core_r.at[p])
        for d in (1, 2, 3):
            to = (x + d) % 4
            x_out[p, d - 1] = (slabs[p, to, :, core] + core_in[p, to]).astype(X_TYPE)
            send(x_out.at[p, d - 1], x_in.at[p, d - 1], x_s.at[p, d - 1], x_r.at[p, d - 1], x_peer[d - 1])
    lax.fori_loop(4, 8, fill, 0)
    for p in range(POLARS):
        total = slabs[p, x, :, core] + core_in[p, x]
        for d in (1, 2, 3):
            arrived(x_in.at[p, d - 1], x_s.at[p, d - 1], x_r.at[p, d - 1])
            total += x_in[p, d - 1].astype(F32)
        z_own[p] = total
        z_out[p] = z_own[p, 1 - zi].astype(Z_TYPE)
        send(z_out.at[p], z_in.at[p], zi_s.at[p], zi_r.at[p], zi_peer)
    lax.fori_loop(8, 16, fill, 0)
    for p in range(POLARS):
        arrived(z_in.at[p], zi_s.at[p], zi_r.at[p])
        held[zh4, zq, y, p] = (z_own[p, zi] + z_in[p].astype(F32)).astype(BF16)
        mine = held.at[zh4, zq, y, p]
        send(mine, mine, z1_s.at[p], z1_r.at[p], z1_peer)

    def to_y(p, d):
        both = held.at[:, (zq - d + 4) % 4, y, p]
        for way in range(2):
            send(both, both, y_s.at[way, d, p], y_r.at[way, d, p], y_peer[way])

    def forward(p, d):
        for way, source in enumerate((y_last, y_next)):
            got = held.at[:, (zq - d + 4) % 4, source, p]
            arrived(got, y_s.at[way, d, p], y_r.at[way, d, p])
            half = held.at[:, (zq - d + 4) % 4, source, p, way]
            send(half, half, f_s.at[way, d, p], f_r.at[way, d, p], y_peer[way])

    for p in range(POLARS):
        theirs = held.at[1 - zh4, zq, y, p]
        arrived(theirs, z1_s.at[p], z1_r.at[p])
        both = held.at[:, zq, y, p]
        for d in (1, 2, 3):
            send(both, both, z2_s.at[d - 1, p], z2_r.at[d - 1, p], z2_peer[d - 1])
        to_y(p, 0)
    for d in (1, 2, 3):
        for p in range(POLARS):
            arrived(held.at[:, (zq - d + 4) % 4, y, p], z2_s.at[d - 1, p], z2_r.at[d - 1, p])
            to_y(p, d)
        for p in range(POLARS):
            forward(p, d - 1)
    for p in range(POLARS):
        forward(p, 3)
    y_far = (y + 2) % 4
    for d in range(4):
        for p in range(POLARS):
            for way in range(2):
                half = held.at[:, (zq - d + 4) % 4, y_far, p, way]
                arrived(half, f_s.at[way, d, p], f_r.at[way, d, p])

    right = jnp.concatenate(
        [
            jnp.concatenate([held[:, :, :, p, k].reshape(512, SPECTRA) for p in range(POLARS)], axis=0)
            for k in range(2)
        ],
        axis=1,
    )

    def arrange(step, carry):
        rows = pl.ds(pl.multiple_of(step * 256, 256), 256)
        ordered[rows, :] = jnp.dot(perm[rows, :], right, preferred_element_type=F32).astype(BF16)
        return carry

    lax.fori_loop(0, 4, arrange, 0)
    mine = ordered[pl.ds(pl.multiple_of(group * 32, 32), 32), :]
    turned = jnp.concatenate([mine[:, SPECTRA:], -mine[:, :SPECTRA]], axis=1)
    left = jnp.concatenate([mine, turned], axis=0)
    for step in range(4):
        block = ordered[pl.ds(step * 256, 256), :]
        seen = lax.dot_general(left, block, (((1,), (1,)), ((), ())), preferred_element_type=F32)
        seen = seen * (1.0 / SPECTRA)
        out[0, :, pl.ds(step * 256, 256)] = seen[:32]
        out[1, :, pl.ds(step * 256, 256)] = seen[32:]
    for copy in started:
        copy.wait_send()


def body(voltages, weights, antenna_slot_index, station_order):
    wt = jnp.transpose(weights, (0, 1, 3, 4, 2)).reshape(1024, ANTENNAS)
    vmem = pl.BlockSpec(memory_space=pltpu.VMEM)
    hbm = pl.BlockSpec(memory_space=pltpu.HBM)
    sem = pltpu.SemaphoreType.DMA
    out = pl.pallas_call(
        kernel,
        out_shape=jax.ShapeDtypeStruct((2, 32, 1024), F32),
        in_specs=[hbm, hbm, hbm, hbm],
        out_specs=vmem,
        scratch_shapes=[
            pltpu.VMEM((STATIONS, SLOTS), I32),
            pltpu.VMEM((1, 512), I32),
            pltpu.VMEM((2, 2, STATIONS, SLOTS, CHANNELS, SPECTRA), BF16),
            pltpu.VMEM((1024, ANTENNAS), BF16),
            pltpu.VMEM((1024, 256), BF16),
            pltpu.VMEM((1024, SPECTRA), F32),
            pltpu.VMEM((2, 4, 2, 2, STATIONS, SPECTRA), F32),
            pltpu.VMEM((2, 3, 2, 2, STATIONS, SPECTRA), X_TYPE),
            pltpu.VMEM((2, 3, 2, 2, STATIONS, SPECTRA), X_TYPE),
            pltpu.VMEM((2, 2, 2, STATIONS, SPECTRA), F32),
            pltpu.VMEM((2, 2, STATIONS, SPECTRA), Z_TYPE),
            pltpu.VMEM((2, 2, STATIONS, SPECTRA), Z_TYPE),
            pltpu.VMEM((2, 4, 4, 2, 2, STATIONS, SPECTRA), BF16),
            pltpu.VMEM((1024, 1024), BF16),
            pltpu.VMEM((1024, 256), BF16),
            sem((2,)), sem((2, 2)), sem,
            sem((2,)), sem((2,)),
            sem((2, 3)), sem((2, 3)),
            sem((2,)), sem((2,)),
            sem((2,)), sem((2,)),
            sem((3, 2)), sem((3, 2)),
            sem((2, 4, 2)), sem((2, 4, 2)),
            sem((2, 4, 2)), sem((2, 4, 2)),
        ],
        compiler_params=pltpu.CompilerParams(
            collective_id=0, has_side_effects=True, vmem_limit_bytes=56 * 2**20
        ),
    )(voltages, wt, antenna_slot_index, station_order.reshape(1, 512))
    return out[None]


def solution(mesh):
    in_specs = (
        P(None, "sgroup", "tile", None, None, None),
        P(None, "sgroup", None, None, None),
        P("sgroup", "tile"),
        P(),
    )
    out_specs = P("tile", None, "sgroup", None)
    return jax.shard_map(body, mesh=mesh, in_specs=in_specs, out_specs=out_specs, check_vma=False)
```

time: 142 us -> 52.6 us (0.37)
  the two profiles are of different devices: /device:TPU:1 before, /device:TPU:2 now
where the time goes in v1:
time: 52.6 us; the launch traced here: 52.5 us
  Pallas kernels  50.8 us (97%)
  local copies, waits for them, and re-layouts  1.67 us (3%)
    pallas_call x1, Pallas kernels, body(): pl.pallas_call(kernel, out_shape=jax.ShapeDtypeStruct((2, 32, 1024), F32)...  50.8 us
    unnamed x1, local copies, waits for them, and re-layouts  1.67 us

profile of v1, /device:TPU:2, one launch (start us, length us, event | category | flops | bytes accessed | tf_op | source)
XLA Modules:
  0.0 52.5 jit_solution(1697048871445292088)
XLA Ops:
  0.0 50.8 %shard_map.46 = f32[2,32,1024]{2,1,0:T(8,128)} custom-call(bf16[2,16,16,2,16,128]{5,4,3,2,1,0:T(8,128)(2,1)} %volt.1, bf16[1024,256]{1,0:T(8,128)(2,1)} %bitcast.6, s32[16,16]{1,0:T(8,128)} %idx_in.1, s32[1,512]{1,0:T(1,128)} %bitcast.7), custom_call_target="tpu_custom_call" | custom-call | tf_op jit(solution)/shard_map/pallas_call | solution.py:220
  50.8 1.7 %copy.6 = f32[1,2,32,1024]{3,2,1,0:T(8,128)} copy(f32[1,2,32,1024]{3,2,1,0:T(8,128)} %bitcast.5) | data formatting | bytes 524288

commit v2 on v1

--- a/solution.py
+++ b/solution.py
@@ -9,7 +9,7 @@
 
 MESH = pl.DeviceIdType.MESH
 F32, BF16, I32 = jnp.float32, jnp.bfloat16, jnp.int32
-X_TYPE, Z_TYPE = BF16, F32
+X_TYPE = F32
 STATIONS, SLOTS, POLARS, CHANNELS, SPECTRA, ANTENNAS = 16, 16, 2, 16, 128, 256
 
 
@@ -24,10 +24,11 @@
 def kernel(
     volt, wt, idx_in, order_in, out,
     idx, order, vbuf, wbuf, wexp, part, core_in, x_out, x_in, z_own, z_out, z_in, held, perm, ordered,
-    i_sem, v_sem, w_sem, core_s, core_r, x_s, x_r, zi_s, zi_r, z1_s, z1_r, z2_s, z2_r, y_s, y_r, f_s, f_r,
+    i_sem, v_sem, w_sem, core_s, core_r, x_s, x_r, zi_s, zi_r, y_s, y_r,
 ):
     group, tile = lax.axis_index("sgroup"), lax.axis_index("tile")
-    zh4, zq, y = group // 16, (group // 4) % 4, group % 4
+    z, y = group // 4, group % 4
+    zh, par = z // 2, z % 2
     x, zi, core = tile // 4, (tile // 2) % 2, tile % 2
 
     def at(g, t):
@@ -35,14 +36,17 @@
 
     sibling = at(group, x * 4 + zi * 2 + (1 - core))
     x_peer = [at(group, ((x + d) % 4) * 4 + zi * 2 + core) for d in (1, 2, 3)]
-    zi_peer = at(group, x * 4 + (1 - zi) * 2 + core)
-    z1_peer = at((1 - zh4) * 16 + zq * 4 + y, tile)
-    z2_peer = [at(zh4 * 16 + ((zq + d) % 4) * 4 + y, tile) for d in (1, 2, 3)]
-    y_next, y_last = (y + 1) % 4, (y + 3) % 4
-    y_peer = [at(zh4 * 16 + zq * 4 + y_next, tile), at(zh4 * 16 + zq * 4 + y_last, tile)]
+    z_steps = [(1, 0), (0, 2), (1, 2), (0, 1), (1, 1), (0, 3), (1, 3)]
+    half_of = (zi, 1 - zi)
+    z_peer = [
+        at((((zh + d) % 4) * 2 + par) * 4 + y, x * 4 + half_of[h] * 2 + core) for h, d in z_steps
+    ]
+    y_steps = [(1, 0), (0, 1), (0, 3), (0, 2), (1, 1), (1, 3), (1, 2)]
+    par_of = (par, 1 - par)
+    y_peer = [at((zh * 2 + par_of[h]) * 4 + (y + d) % 4, tile) for h, d in y_steps]
 
     barrier = pltpu.get_barrier_semaphore()
-    partners = [sibling, *x_peer, zi_peer, z1_peer, *z2_peer, *y_peer]
+    partners = [sibling, *x_peer, *z_peer, *y_peer]
 
     small = [
         pltpu.make_async_copy(idx_in, idx, i_sem.at[0]),
@@ -63,7 +67,6 @@
 
     for partner in partners:
         pl.semaphore_signal(barrier, inc=1, device_id=partner, device_id_type=MESH)
-    pl.semaphore_wait(barrier, len(partners))
 
     started = []
 
@@ -103,6 +106,7 @@
 
     lax.fori_loop(0, 4, pick, 0)
 
+    pl.semaphore_wait(barrier, len(partners))
     slabs = part.reshape(POLARS, 4, 2, 2, 2, STATIONS, SPECTRA)
     for p in range(POLARS):
         for q in range(2):
@@ -128,62 +132,38 @@
         perm[pl.ds(pl.multiple_of(step * 64, 64), 64), :] = as_bf16(rows == lane_row)
         return carry
 
-    lax.fori_loop(0, 4, fill, 0)
     for p in range(POLARS):
         arrived(core_in.at[p], core_s.at[p], core_r.at[p])
         for d in (1, 2, 3):
             to = (x + d) % 4
             x_out[p, d - 1] = (slabs[p, to, :, core] + core_in[p, to]).astype(X_TYPE)
             send(x_out.at[p, d - 1], x_in.at[p, d - 1], x_s.at[p, d - 1], x_r.at[p, d - 1], x_peer[d - 1])
-    lax.fori_loop(4, 8, fill, 0)
+    lax.fori_loop(0, 8, fill, 0)
     for p in range(POLARS):
         total = slabs[p, x, :, core] + core_in[p, x]
         for d in (1, 2, 3):
             arrived(x_in.at[p, d - 1], x_s.at[p, d - 1], x_r.at[p, d - 1])
             total += x_in[p, d - 1].astype(F32)
         z_own[p] = total
-        z_out[p] = z_own[p, 1 - zi].astype(Z_TYPE)
-        send(z_out.at[p], z_in.at[p], zi_s.at[p], zi_r.at[p], zi_peer)
+        z_out[p] = total.astype(BF16)
+        for j, (h, d) in enumerate(z_steps):
+            send(z_out.at[p, half_of[h]], z_in.at[p, h, d], zi_s.at[p, j], zi_r.at[p, j], z_peer[j])
     lax.fori_loop(8, 16, fill, 0)
-    for p in range(POLARS):
-        arrived(z_in.at[p], zi_s.at[p], zi_r.at[p])
-        held[zh4, zq, y, p] = (z_own[p, zi] + z_in[p].astype(F32)).astype(BF16)
-        mine = held.at[zh4, zq, y, p]
-        send(mine, mine, z1_s.at[p], z1_r.at[p], z1_peer)
-
-    def to_y(p, d):
-        both = held.at[:, (zq - d + 4) % 4, y, p]
-        for way in range(2):
-            send(both, both, y_s.at[way, d, p], y_r.at[way, d, p], y_peer[way])
-
-    def forward(p, d):
-        for way, source in enumerate((y_last, y_next)):
-            got = held.at[:, (zq - d + 4) % 4, source, p]
-            arrived(got, y_s.at[way, d, p], y_r.at[way, d, p])
-            half = held.at[:, (zq - d + 4) % 4, source, p, way]
-            send(half, half, f_s.at[way, d, p], f_r.at[way, d, p], y_peer[way])
-
-    for p in range(POLARS):
-        theirs = held.at[1 - zh4, zq, y, p]
-        arrived(theirs, z1_s.at[p], z1_r.at[p])
-        both = held.at[:, zq, y, p]
-        for d in (1, 2, 3):
-            send(both, both, z2_s.at[d - 1, p], z2_r.at[d - 1, p], z2_peer[d - 1])
-        to_y(p, 0)
-    for d in (1, 2, 3):
+    for d in (2, 1, 3, 0):
+        source = (zh - d + 4) % 4
         for p in range(POLARS):
-            arrived(held.at[:, (zq - d + 4) % 4, y, p], z2_s.at[d - 1, p], z2_r.at[d - 1, p])
-            to_y(p, d)
-        for p in range(POLARS):
-            forward(p, d - 1)
-    for p in range(POLARS):
-        forward(p, 3)
-    y_far = (y + 2) % 4
-    for d in range(4):
-        for p in range(POLARS):
-            for way in range(2):
-                half = held.at[:, (zq - d + 4) % 4, y_far, p, way]
-                arrived(half, f_s.at[way, d, p], f_r.at[way, d, p])
+            for j, (h, step) in enumerate(z_steps):
+                if step == d:
+                    arrived(z_in.at[p, h, d], zi_s.at[p, j], zi_r.at[p, j])
+            first = z_own[p, zi] if d == 0 else z_in[p, 0, d].astype(F32)
+            held[source, par, y, p] = (first + z_in[p, 1, d].astype(F32)).astype(BF16)
+        mine = held.at[source, par, y]
+        for j in range(7):
+            send(mine, mine, y_s.at[d, j], y_r.at[d, j], y_peer[j])
+    for d in (2, 1, 3, 0):
+        source = (zh - d + 4) % 4
+        for j, (h, step) in enumerate(y_steps):
+            arrived(held.at[source, par_of[h], (y - step + 4) % 4], y_s.at[d, j], y_r.at[d, j])
 
     right = jnp.concatenate(
         [
@@ -233,19 +213,16 @@
             pltpu.VMEM((2, 3, 2, 2, STATIONS, SPECTRA), X_TYPE),
             pltpu.VMEM((2, 3, 2, 2, STATIONS, SPECTRA), X_TYPE),
             pltpu.VMEM((2, 2, 2, STATIONS, SPECTRA), F32),
-            pltpu.VMEM((2, 2, STATIONS, SPECTRA), Z_TYPE),
-            pltpu.VMEM((2, 2, STATIONS, SPECTRA), Z_TYPE),
-            pltpu.VMEM((2, 4, 4, 2, 2, STATIONS, SPECTRA), BF16),
+            pltpu.VMEM((2, 2, 2, STATIONS, SPECTRA), BF16),
+            pltpu.VMEM((2, 2, 4, 2, STATIONS, SPECTRA), BF16),
+            pltpu.VMEM((4, 2, 4, 2, 2, STATIONS, SPECTRA), BF16),
             pltpu.VMEM((1024, 1024), BF16),
             pltpu.VMEM((1024, 256), BF16),
             sem((2,)), sem((2, 2)), sem,
             sem((2,)), sem((2,)),
             sem((2, 3)), sem((2, 3)),
-            sem((2,)), sem((2,)),
-            sem((2,)), sem((2,)),
-            sem((3, 2)), sem((3, 2)),
-            sem((2, 4, 2)), sem((2, 4, 2)),
-            sem((2, 4, 2)), sem((2, 4, 2)),
+            sem((2, 7)), sem((2, 7)),
+            sem((4, 7)), sem((4, 7)),
         ],
         compiler_params=pltpu.CompilerParams(
             collective_id=0, has_side_effects=True, vmem_limit_bytes=56 * 2**20

time: 52.6 us -> 45.1 us (0.86)
  the two profiles are of different devices: /device:TPU:2 before, /device:TPU:1 now
where the time goes in v2:
time: 45.1 us; the launch traced here: 45 us
  Pallas kernels  43.3 us (96%)
  local copies, waits for them, and re-layouts  1.67 us (4%)
    pallas_call x1, Pallas kernels, body(): pl.pallas_call(kernel, out_shape=jax.ShapeDtypeStruct((2, 32, 1024), F32)...  43.3 us
    unnamed x1, local copies, waits for them, and re-layouts  1.67 us

profile of v2, /device:TPU:1, one launch (start us, length us, event | category | flops | bytes accessed | tf_op | source)
XLA Modules:
  0.0 45.0 jit_solution(13927260153242787535)
XLA Ops:
  0.0 43.3 %shard_map.46 = f32[2,32,1024]{2,1,0:T(8,128)} custom-call(bf16[2,16,16,2,16,128]{5,4,3,2,1,0:T(8,128)(2,1)} %volt.1, bf16[1024,256]{1,0:T(8,128)(2,1)} %bitcast.6, s32[16,16]{1,0:T(8,128)} %idx_in.1, s32[1,512]{1,0:T(1,128)} %bitcast.7), custom_call_target="tpu_custom_call" | custom-call | tf_op jit(solution)/shard_map/pallas_call | solution.py:200
  43.3 1.7 %copy.6 = f32[1,2,32,1024]{3,2,1,0:T(8,128)} copy(f32[1,2,32,1024]{3,2,1,0:T(8,128)} %bitcast.5) | data formatting | bytes 524288

commit v3 on v2

--- a/solution.py
+++ b/solution.py
@@ -9,7 +9,6 @@
 
 MESH = pl.DeviceIdType.MESH
 F32, BF16, I32 = jnp.float32, jnp.bfloat16, jnp.int32
-X_TYPE = F32
 STATIONS, SLOTS, POLARS, CHANNELS, SPECTRA, ANTENNAS = 16, 16, 2, 16, 128, 256
 
 
@@ -23,8 +22,8 @@
 
 def kernel(
     volt, wt, idx_in, order_in, out,
-    idx, order, vbuf, wbuf, wexp, part, core_in, x_out, x_in, z_own, z_out, z_in, held, perm, ordered,
-    i_sem, v_sem, w_sem, core_s, core_r, x_s, x_r, zi_s, zi_r, y_s, y_r,
+    idx, order, vbuf, wbuf, wexp, part, core_in, x_out, x_in, z_own, z_out, z_in, held, perm, summed, ordered,
+    i_sem, v_sem, w_sem, core_s, core_r, x_s, x_r, z_s, z_r, ready, y_s, y_r,
 ):
     group, tile = lax.axis_index("sgroup"), lax.axis_index("tile")
     z, y = group // 4, group % 4
@@ -36,17 +35,17 @@
 
     sibling = at(group, x * 4 + zi * 2 + (1 - core))
     x_peer = [at(group, ((x + d) % 4) * 4 + zi * 2 + core) for d in (1, 2, 3)]
-    z_steps = [(1, 0), (0, 2), (1, 2), (0, 1), (1, 1), (0, 3), (1, 3)]
-    half_of = (zi, 1 - zi)
     z_peer = [
-        at((((zh + d) % 4) * 2 + par) * 4 + y, x * 4 + half_of[h] * 2 + core) for h, d in z_steps
+        [at((e * 2 + par) * 4 + y, x * 4 + half * 2 + core) for e in range(4)] for half in range(2)
     ]
-    y_steps = [(1, 0), (0, 1), (0, 3), (0, 2), (1, 1), (1, 3), (1, 2)]
-    par_of = (par, 1 - par)
-    y_peer = [at((zh * 2 + par_of[h]) * 4 + (y + d) % 4, tile) for h, d in y_steps]
+    near_peer = [at((((zh + d) % 4) * 2 + par) * 4 + y, tile) for d in (1, 2, 3)]
+    far_peer = [at((e * 2 + par) * 4 + y, x * 4 + (1 - zi) * 2 + core) for e in range(4)]
+    pair_peer = at((zh * 2 + 1 - par) * 4 + y, tile)
+    y_steps = [(e, d) for e in (0, 1) for d in (1, 3, 2)]
+    y_peer = [at((zh * 2 + e) * 4 + (y + d) % 4, tile) for e, d in y_steps]
 
     barrier = pltpu.get_barrier_semaphore()
-    partners = [sibling, *x_peer, *z_peer, *y_peer]
+    partners = [sibling, *x_peer, *near_peer, pair_peer, *y_peer]
 
     small = [
         pltpu.make_async_copy(idx_in, idx, i_sem.at[0]),
@@ -68,6 +67,11 @@
     for partner in partners:
         pl.semaphore_signal(barrier, inc=1, device_id=partner, device_id_type=MESH)
 
+    @pl.when(zi == 0)
+    def _():
+        for partner in far_peer:
+            pl.semaphore_signal(barrier, inc=1, device_id=partner, device_id_type=MESH)
+
     started = []
 
     def send(src, dst, s, r, device):
@@ -76,6 +80,12 @@
         )
         copy.start()
         started.append(copy)
+
+    def to_z(h, p, e):
+        return pltpu.make_async_remote_copy(
+            src_ref=z_out.at[h, p], dst_ref=z_in.at[p, zi, zh], send_sem=z_s.at[h, p, e],
+            recv_sem=z_r.at[p, zi, zh], device_id=z_peer[h][e], device_id_type=MESH,
+        )
 
     def arrived(dst, s, r):
         pltpu.make_async_remote_copy(
@@ -106,7 +116,13 @@
 
     lax.fori_loop(0, 4, pick, 0)
 
-    pl.semaphore_wait(barrier, len(partners))
+    pl.semaphore_wait(barrier, len(partners) + 4 * zi)
+
+    @pl.when(zi == 1)
+    def _():
+        for partner in far_peer:
+            pl.semaphore_signal(ready, inc=1, device_id=partner, device_id_type=MESH)
+
     slabs = part.reshape(POLARS, 4, 2, 2, 2, STATIONS, SPECTRA)
     for p in range(POLARS):
         for q in range(2):
@@ -123,62 +139,87 @@
                 imag = both[:16, SPECTRA:] + both[16:, :SPECTRA]
                 part[pl.ds(p * 512 + s, 16, stride=32), :] = real
                 part[pl.ds(p * 512 + 16 + s, 16, stride=32), :] = imag
-        send(slabs.at[p, :, :, 1 - core], core_in.at[p], core_s.at[p], core_r.at[p], sibling)
-
-    lane_row = jnp.concatenate([order[...] * 2, order[...] * 2 + 1], axis=1)
+        for h in range(2):
+            theirs = slabs.at[p, :, h, 1 - core]
+            send(theirs, core_in.at[h, p], core_s.at[h, p], core_r.at[h, p], sibling)
 
     def fill(step, carry):
-        rows = step * 64 + iota((64, 1024), 0)
-        perm[pl.ds(pl.multiple_of(step * 64, 64), 64), :] = as_bf16(rows == lane_row)
+        rows = (step % 8) * 128 + iota((128, 256), 0)
+        block = order[:, pl.ds(pl.multiple_of((step // 8) * 128, 128), 128)]
+        lane_row = jnp.concatenate([block * 2, block * 2 + 1], axis=1)
+        perm[step // 8, pl.ds(pl.multiple_of((step % 8) * 128, 128), 128), :] = as_bf16(rows == lane_row)
         return carry
 
-    for p in range(POLARS):
-        arrived(core_in.at[p], core_s.at[p], core_r.at[p])
-        for d in (1, 2, 3):
-            to = (x + d) % 4
-            x_out[p, d - 1] = (slabs[p, to, :, core] + core_in[p, to]).astype(X_TYPE)
-            send(x_out.at[p, d - 1], x_in.at[p, d - 1], x_s.at[p, d - 1], x_r.at[p, d - 1], x_peer[d - 1])
-    lax.fori_loop(0, 8, fill, 0)
-    for p in range(POLARS):
-        total = slabs[p, x, :, core] + core_in[p, x]
-        for d in (1, 2, 3):
-            arrived(x_in.at[p, d - 1], x_s.at[p, d - 1], x_r.at[p, d - 1])
-            total += x_in[p, d - 1].astype(F32)
-        z_own[p] = total
-        z_out[p] = total.astype(BF16)
-        for j, (h, d) in enumerate(z_steps):
-            send(z_out.at[p, half_of[h]], z_in.at[p, h, d], zi_s.at[p, j], zi_r.at[p, j], z_peer[j])
-    lax.fori_loop(8, 16, fill, 0)
-    for d in (2, 1, 3, 0):
+    for h in range(2):
+        for p in range(POLARS):
+            arrived(core_in.at[h, p], core_s.at[h, p], core_r.at[h, p])
+            for d in (1, 2, 3):
+                to = (x + d) % 4
+                x_out[h, p, d - 1] = slabs[p, to, h, core] + core_in[h, p, to]
+                send(
+                    x_out.at[h, p, d - 1], x_in.at[h, p, d - 1],
+                    x_s.at[h, p, d - 1], x_r.at[h, p, d - 1], x_peer[d - 1],
+                )
+        lax.fori_loop(h * 16, h * 16 + 16, fill, 0)
+        for p in range(POLARS):
+            total = slabs[p, x, h, core] + core_in[h, p, x]
+            for d in (1, 2, 3):
+                arrived(x_in.at[h, p, d - 1], x_s.at[h, p, d - 1], x_r.at[h, p, d - 1])
+                total += x_in[h, p, d - 1]
+            z_out[h, p] = total.astype(BF16)
+
+            @pl.when(zi == h)
+            def _():
+                z_own[p] = total
+
+            if h == 1 and p == 0:
+
+                @pl.when(zi == 0)
+                def _():
+                    pl.semaphore_wait(ready, 4)
+
+            for e in range(4):
+
+                @pl.when(jnp.logical_or(zi != h, zh != e))
+                def _():
+                    to_z(h, p, e).start()
+
+    for d in (1, 2, 3, 0):
         source = (zh - d + 4) % 4
         for p in range(POLARS):
-            for j, (h, step) in enumerate(z_steps):
-                if step == d:
-                    arrived(z_in.at[p, h, d], zi_s.at[p, j], zi_r.at[p, j])
-            first = z_own[p, zi] if d == 0 else z_in[p, 0, d].astype(F32)
-            held[source, par, y, p] = (first + z_in[p, 1, d].astype(F32)).astype(BF16)
+            if d == 0:
+                first = z_own[p]
+            else:
+                arrived(z_in.at[p, zi, source], z_s.at[0, p, d], z_r.at[p, zi, source])
+                first = z_in[p, zi, source].astype(F32)
+            arrived(z_in.at[p, 1 - zi, source], z_s.at[1, p, d], z_r.at[p, 1 - zi, source])
+            held[source, par, y, p] = (first + z_in[p, 1 - zi, source].astype(F32)).astype(BF16)
         mine = held.at[source, par, y]
-        for j in range(7):
-            send(mine, mine, y_s.at[d, j], y_r.at[d, j], y_peer[j])
-    for d in (2, 1, 3, 0):
+        send(mine, mine, y_s.at[d, 6], y_r.at[d, par, 0], pair_peer)
+        for j, (_, step) in enumerate(y_steps):
+            send(mine, mine, y_s.at[d, j], y_r.at[d, par, step], y_peer[j])
+
+    for d in (1, 2, 3, 0):
         source = (zh - d + 4) % 4
-        for j, (h, step) in enumerate(y_steps):
-            arrived(held.at[source, par_of[h], (y - step + 4) % 4], y_s.at[d, j], y_r.at[d, j])
-
-    right = jnp.concatenate(
-        [
-            jnp.concatenate([held[:, :, :, p, k].reshape(512, SPECTRA) for p in range(POLARS)], axis=0)
-            for k in range(2)
-        ],
-        axis=1,
-    )
-
-    def arrange(step, carry):
-        rows = pl.ds(pl.multiple_of(step * 256, 256), 256)
-        ordered[rows, :] = jnp.dot(perm[rows, :], right, preferred_element_type=F32).astype(BF16)
-        return carry
-
-    lax.fori_loop(0, 4, arrange, 0)
+        arrived(held.at[source, 1 - par, y], y_s.at[d, 6], y_r.at[d, 1 - par, 0])
+        for j, (e, step) in enumerate(y_steps):
+            arrived(held.at[source, e, (y - step + 4) % 4], y_s.at[d, j], y_r.at[d, e, step])
+        right = jnp.concatenate(
+            [
+                jnp.concatenate([held[source, :, :, p, k].reshape(128, SPECTRA) for p in range(POLARS)], axis=0)
+                for k in range(2)
+            ],
+            axis=1,
+        )
+        for step in range(4):
+            rows = pl.ds(step * 256, 256)
+            got = jnp.dot(perm[source, rows, :], right, preferred_element_type=F32)
+            if d == 1:
+                summed[rows, :] = got
+            elif d > 0:
+                summed[rows, :] += got
+            else:
+                ordered[rows, :] = (summed[rows, :] + got).astype(BF16)
     mine = ordered[pl.ds(pl.multiple_of(group * 32, 32), 32), :]
     turned = jnp.concatenate([mine[:, SPECTRA:], -mine[:, :SPECTRA]], axis=1)
     left = jnp.concatenate([mine, turned], axis=0)
@@ -190,6 +231,13 @@
         out[1, :, pl.ds(step * 256, 256)] = seen[32:]
     for copy in started:
         copy.wait_send()
+    for h in range(2):
+        for p in range(POLARS):
+            for e in range(4):
+
+                @pl.when(jnp.logical_or(zi != h, zh != e))
+                def _():
+                    to_z(h, p, e).wait_send()
 
 
 def body(voltages, weights, antenna_slot_index, station_order):
@@ -209,20 +257,21 @@
             pltpu.VMEM((1024, ANTENNAS), BF16),
             pltpu.VMEM((1024, 256), BF16),
             pltpu.VMEM((1024, SPECTRA), F32),
-            pltpu.VMEM((2, 4, 2, 2, STATIONS, SPECTRA), F32),
-            pltpu.VMEM((2, 3, 2, 2, STATIONS, SPECTRA), X_TYPE),
-            pltpu.VMEM((2, 3, 2, 2, STATIONS, SPECTRA), X_TYPE),
-            pltpu.VMEM((2, 2, 2, STATIONS, SPECTRA), F32),
+            pltpu.VMEM((2, 2, 4, 2, STATIONS, SPECTRA), F32),
+            pltpu.VMEM((2, 2, 3, 2, STATIONS, SPECTRA), F32),
+            pltpu.VMEM((2, 2, 3, 2, STATIONS, SPECTRA), F32),
+            pltpu.VMEM((2, 2, STATIONS, SPECTRA), F32),
             pltpu.VMEM((2, 2, 2, STATIONS, SPECTRA), BF16),
             pltpu.VMEM((2, 2, 4, 2, STATIONS, SPECTRA), BF16),
             pltpu.VMEM((4, 2, 4, 2, 2, STATIONS, SPECTRA), BF16),
-            pltpu.VMEM((1024, 1024), BF16),
+            pltpu.VMEM((4, 1024, 256), BF16),
+            pltpu.VMEM((1024, 256), F32),
             pltpu.VMEM((1024, 256), BF16),
             sem((2,)), sem((2, 2)), sem,
-            sem((2,)), sem((2,)),
-            sem((2, 3)), sem((2, 3)),
-            sem((2, 7)), sem((2, 7)),
-            sem((4, 7)), sem((4, 7)),
+            sem((2, 2)), sem((2, 2)),
+            sem((2, 2, 3)), sem((2, 2, 3)),
+            sem((2, 2, 4)), sem((2, 2, 4)), pltpu.SemaphoreType.REGULAR,
+            sem((4, 7)), sem((4, 2, 4)),
         ],
         compiler_params=pltpu.CompilerParams(
             collective_id=0, has_side_effects=True, vmem_limit_bytes=56 * 2**20

time: 45.1 us -> 41.5 us (0.920)
  Pallas kernels: 43.3 us -> 39.7 us
    pallas_call x1, Pallas kernels: 43.3 us -> 39.7 us  [body(): pl.pallas_call(kernel, out_shape=jax.ShapeDtypeStruct((2, 32, 1024), F32)...]
where the time goes in v3:
time: 41.5 us; the launch traced here: 41.4 us
  Pallas kernels  39.7 us (96%)
  local copies, waits for them, and re-layouts  1.67 us (4%)
    pallas_call x1, Pallas kernels, body(): pl.pallas_call(kernel, out_shape=jax.ShapeDtypeStruct((2, 32, 1024), F32)...  39.7 us
    unnamed x1, local copies, waits for them, and re-layouts  1.67 us

profile of v3, /device:TPU:1, one launch (start us, length us, event | category | flops | bytes accessed | tf_op | source)
XLA Modules:
  0.0 41.4 jit_solution(9506453912506423974)
XLA Ops:
  0.0 39.7 %shard_map.46 = f32[2,32,1024]{2,1,0:T(8,128)} custom-call(bf16[2,16,16,2,16,128]{5,4,3,2,1,0:T(8,128)(2,1)} %volt.1, bf16[1024,256]{1,0:T(8,128)(2,1)} %bitcast.6, s32[16,16]{1,0:T(8,128)} %idx_in.1, s32[1,512]{1,0:T(1,128)} %bitcast.7), custom_call_target="tpu_custom_call" | custom-call | tf_op jit(solution)/shard_map/pallas_call | solution.py:248
  39.7 1.7 %copy.6 = f32[1,2,32,1024]{3,2,1,0:T(8,128)} copy(f32[1,2,32,1024]{3,2,1,0:T(8,128)} %bitcast.5) | data formatting | bytes 524288

commit v4 on v3

--- a/solution.py
+++ b/solution.py
@@ -22,7 +22,7 @@
 
 def kernel(
     volt, wt, idx_in, order_in, out,
-    idx, order, vbuf, wbuf, wexp, part, core_in, x_out, x_in, z_own, z_out, z_in, held, perm, summed, ordered,
+    idx, order, vbuf, wbuf, wexp, part, core_in, x_out, x_in, z_own, z_out, near_in, far_in, held, perm, summed, ordered,
     i_sem, v_sem, w_sem, core_s, core_r, x_s, x_r, z_s, z_r, ready, y_s, y_r,
 ):
     group, tile = lax.axis_index("sgroup"), lax.axis_index("tile")
@@ -36,16 +36,15 @@
     sibling = at(group, x * 4 + zi * 2 + (1 - core))
     x_peer = [at(group, ((x + d) % 4) * 4 + zi * 2 + core) for d in (1, 2, 3)]
     z_peer = [
-        [at((e * 2 + par) * 4 + y, x * 4 + half * 2 + core) for e in range(4)] for half in range(2)
+        [at((e * 2 + 1 - par) * 4 + y, x * 4 + half * 2 + core) for e in range(4)] for half in (zi, 1 - zi)
     ]
-    near_peer = [at((((zh + d) % 4) * 2 + par) * 4 + y, tile) for d in (1, 2, 3)]
-    far_peer = [at((e * 2 + par) * 4 + y, x * 4 + (1 - zi) * 2 + core) for e in range(4)]
+    near_peer, far_peer = z_peer
     pair_peer = at((zh * 2 + 1 - par) * 4 + y, tile)
     y_steps = [(e, d) for e in (0, 1) for d in (1, 3, 2)]
     y_peer = [at((zh * 2 + e) * 4 + (y + d) % 4, tile) for e, d in y_steps]
 
     barrier = pltpu.get_barrier_semaphore()
-    partners = [sibling, *x_peer, *near_peer, pair_peer, *y_peer]
+    partners = [sibling, *x_peer, pair_peer, *y_peer]
 
     small = [
         pltpu.make_async_copy(idx_in, idx, i_sem.at[0]),
@@ -69,7 +68,7 @@
 
     @pl.when(zi == 0)
     def _():
-        for partner in far_peer:
+        for partner in near_peer + far_peer:
             pl.semaphore_signal(barrier, inc=1, device_id=partner, device_id_type=MESH)
 
     started = []
@@ -81,10 +80,10 @@
         copy.start()
         started.append(copy)
 
-    def to_z(h, p, e):
+    def to_z(far, e):
         return pltpu.make_async_remote_copy(
-            src_ref=z_out.at[h, p], dst_ref=z_in.at[p, zi, zh], send_sem=z_s.at[h, p, e],
-            recv_sem=z_r.at[p, zi, zh], device_id=z_peer[h][e], device_id_type=MESH,
+            src_ref=(z_own, z_out)[far], dst_ref=(near_in, far_in)[far].at[zh], send_sem=z_s.at[far, e],
+            recv_sem=z_r.at[far, zh], device_id=z_peer[far][e], device_id_type=MESH,
         )
 
     def arrived(dst, s, r):
@@ -104,19 +103,19 @@
     unfold = as_bf16(iota((lanes, lanes), 0) % SLOTS == iota((lanes, lanes), 1) // CHANNELS)
     w_copy.wait()
 
-    def pick(step, carry):
+    def pick(step):
         kept = (step % 2) * 8 + iota((256, lanes), 0) // 32 == iota((256, lanes), 1) // SLOTS
-        block = wbuf[pl.ds(pl.multiple_of(step * 256, 256), 256), :]
+        block = wbuf[pl.ds(step * 256, 256), :]
         got = jnp.dot(block, onehot, preferred_element_type=F32)
         got = jnp.where(kept, got, 0.0).astype(BF16)
         got = jnp.dot(got, unfold, preferred_element_type=F32)
         same = iota((256, lanes), 0) % CHANNELS == iota((256, lanes), 1) % CHANNELS
-        wexp[pl.ds(pl.multiple_of(step * 256, 256), 256), :] = jnp.where(same, got, 0.0).astype(BF16)
-        return carry
-
-    lax.fori_loop(0, 4, pick, 0)
-
-    pl.semaphore_wait(barrier, len(partners) + 4 * zi)
+        wexp[pl.ds(step * 256, 256), :] = jnp.where(same, got, 0.0).astype(BF16)
+
+    for step in range(4):
+        pick(step)
+
+    pl.semaphore_wait(barrier, len(partners) + 4)
 
     @pl.when(zi == 1)
     def _():
@@ -166,44 +165,52 @@
             for d in (1, 2, 3):
                 arrived(x_in.at[h, p, d - 1], x_s.at[h, p, d - 1], x_r.at[h, p, d - 1])
                 total += x_in[h, p, d - 1]
-            z_out[h, p] = total.astype(BF16)
 
             @pl.when(zi == h)
             def _():
                 z_own[p] = total
 
-            if h == 1 and p == 0:
-
-                @pl.when(zi == 0)
-                def _():
-                    pl.semaphore_wait(ready, 4)
-
+            @pl.when(zi != h)
+            def _():
+                z_out[p] = total.astype(BF16)
+
+        if h == 1:
+
+            @pl.when(zi == 0)
+            def _():
+                pl.semaphore_wait(ready, 4)
+                for partner in far_peer:
+                    pl.semaphore_signal(ready, inc=1, device_id=partner, device_id_type=MESH)
+
+            @pl.when(zi == 1)
+            def _():
+                pl.semaphore_wait(ready, 4)
+
+        @pl.when(zi == h)
+        def _():
             for e in range(4):
-
-                @pl.when(jnp.logical_or(zi != h, zh != e))
-                def _():
-                    to_z(h, p, e).start()
+                to_z(0, e).start()
+
+        @pl.when(zi != h)
+        def _():
+            for e in range(4):
+                to_z(1, e).start()
 
     for d in (1, 2, 3, 0):
         source = (zh - d + 4) % 4
-        for p in range(POLARS):
-            if d == 0:
-                first = z_own[p]
-            else:
-                arrived(z_in.at[p, zi, source], z_s.at[0, p, d], z_r.at[p, zi, source])
-                first = z_in[p, zi, source].astype(F32)
-            arrived(z_in.at[p, 1 - zi, source], z_s.at[1, p, d], z_r.at[p, 1 - zi, source])
-            held[source, par, y, p] = (first + z_in[p, 1 - zi, source].astype(F32)).astype(BF16)
-        mine = held.at[source, par, y]
-        send(mine, mine, y_s.at[d, 6], y_r.at[d, par, 0], pair_peer)
+        arrived(near_in.at[source], z_s.at[0, d], z_r.at[0, source])
+        arrived(far_in.at[source], z_s.at[1, d], z_r.at[1, source])
+        held[source, 1 - par, y] = (near_in[source] + far_in[source].astype(F32)).astype(BF16)
+        mine = held.at[source, 1 - par, y]
+        send(mine, mine, y_s.at[d, 6], y_r.at[d, 1 - par, 0], pair_peer)
         for j, (_, step) in enumerate(y_steps):
-            send(mine, mine, y_s.at[d, j], y_r.at[d, par, step], y_peer[j])
+            send(mine, mine, y_s.at[d, j], y_r.at[d, 1 - par, step], y_peer[j])
 
     for d in (1, 2, 3, 0):
         source = (zh - d + 4) % 4
-        arrived(held.at[source, 1 - par, y], y_s.at[d, 6], y_r.at[d, 1 - par, 0])
+        arrived(held.at[source, par, y], y_s.at[d, 6], y_r.at[d, par, 0])
         for j, (e, step) in enumerate(y_steps):
-            arrived(held.at[source, e, (y - step + 4) % 4], y_s.at[d, j], y_r.at[d, e, step])
+            arrived(held.at[source, 1 - e, (y - step + 4) % 4], y_s.at[d, j], y_r.at[d, 1 - e, step])
         right = jnp.concatenate(
             [
                 jnp.concatenate([held[source, :, :, p, k].reshape(128, SPECTRA) for p in range(POLARS)], axis=0)
@@ -231,13 +238,9 @@
         out[1, :, pl.ds(step * 256, 256)] = seen[32:]
     for copy in started:
         copy.wait_send()
-    for h in range(2):
-        for p in range(POLARS):
-            for e in range(4):
-
-                @pl.when(jnp.logical_or(zi != h, zh != e))
-                def _():
-                    to_z(h, p, e).wait_send()
+    for far in range(2):
+        for e in range(4):
+            to_z(far, e).wait_send()
 
 
 def body(voltages, weights, antenna_slot_index, station_order):
@@ -261,8 +264,9 @@
             pltpu.VMEM((2, 2, 3, 2, STATIONS, SPECTRA), F32),
             pltpu.VMEM((2, 2, 3, 2, STATIONS, SPECTRA), F32),
             pltpu.VMEM((2, 2, STATIONS, SPECTRA), F32),
-            pltpu.VMEM((2, 2, 2, STATIONS, SPECTRA), BF16),
-            pltpu.VMEM((2, 2, 4, 2, STATIONS, SPECTRA), BF16),
+            pltpu.VMEM((2, 2, STATIONS, SPECTRA), BF16),
+            pltpu.VMEM((4, 2, 2, STATIONS, SPECTRA), F32),
+            pltpu.VMEM((4, 2, 2, STATIONS, SPECTRA), BF16),
             pltpu.VMEM((4, 2, 4, 2, 2, STATIONS, SPECTRA), BF16),
             pltpu.VMEM((4, 1024, 256), BF16),
             pltpu.VMEM((1024, 256), F32),
@@ -270,11 +274,11 @@
             sem((2,)), sem((2, 2)), sem,
             sem((2, 2)), sem((2, 2)),
             sem((2, 2, 3)), sem((2, 2, 3)),
-            sem((2, 2, 4)), sem((2, 2, 4)), pltpu.SemaphoreType.REGULAR,
+            sem((2, 4)), sem((2, 4)), pltpu.SemaphoreType.REGULAR,
             sem((4, 7)), sem((4, 2, 4)),
         ],
         compiler_params=pltpu.CompilerParams(
-            collective_id=0, has_side_effects=True, vmem_limit_bytes=56 * 2**20
+            collective_id=0, has_side_effects=True, vmem_limit_bytes=54700 * 1024
         ),
     )(voltages, wt, antenna_slot_index, station_order.reshape(1, 512))
     return out[None]

time: 41.5 us -> 41 us (0.988)
  Pallas kernels: 39.7 us -> 38.7 us
    pallas_call x1, Pallas kernels: 39.7 us -> 38.7 us  [body(): pl.pallas_call(kernel, out_shape=jax.ShapeDtypeStruct((2, 32, 1024), F32)...]
    unnamed x1 -> x5, local copies, waits for them, and re-layouts: 1.67 us -> 2.08 us
where the time goes in v4:
time: 41 us; the launch traced here: 40.8 us
  Pallas kernels  38.7 us (94%)
  local copies, waits for them, and re-layouts  2.08 us (5%)
    pallas_call x1, Pallas kernels, body(): pl.pallas_call(kernel, out_shape=jax.ShapeDtypeStruct((2, 32, 1024), F32)...  38.7 us
    unnamed x5, local copies, waits for them, and re-layouts  2.08 us

profile of v4, /device:TPU:1, one launch (start us, length us, event | category | flops | bytes accessed | tf_op | source)
XLA Modules:
  0.0 40.8 jit_solution(7537098510731491371)
XLA Ops:
  0.0 0.0 copy-start
  0.0 0.7 %copy-done = s32[16,16]{1,0:T(8,128)S(1)} copy-done((s32[16,16]{1,0:T(8,128)S(1)}, s32[16,16]{1,0:T(8,128)}, u32[]{:S(2)}) %copy-start) | copy-done | bytes 1048
  0.7 0.0 copy-start.1
  0.7 0.7 %copy-done.1 = s32[512]{0:T(512)S(1)} copy-done((s32[512]{0:T(512)S(1)}, s32[512]{0:T(512)}, u32[]{:S(2)}) %copy-start.1) | copy-done | bytes 2072
  1.4 38.7 %shard_map.46 = f32[2,32,1024]{2,1,0:T(8,128)S(1)} custom-call(bf16[2,16,16,2,16,128]{5,4,3,2,1,0:T(8,128)(2,1)} %volt.1, bf16[1024,256]{1,0:T(8,128)(2,1)} %bitcast.7, s32[16,16]{1,0:T(8,128)S(1)} %copy-done, s32[1,512]{1,0:T(1,128)S(1)} %bitcast.6), custom_call_target="tpu_custom_call" | custom-call | tf_op jit(solution)/shard_map/pallas_call | solution.py:251
  40.1 0.7 %copy.6 = f32[1,2,32,1024]{3,2,1,0:T(8,128)} copy(f32[1,2,32,1024]{3,2,1,0:T(8,128)S(1)} %bitcast.5) | data formatting | bytes 524288
Async XLA Ops:
  0.0 0.7 %copy-start = (s32[16,16]{1,0:T(8,128)S(1)}, s32[16,16]{1,0:T(8,128)}, u32[]{:S(2)}) copy-start(s32[16,16]{1,0:T(8,128)} %idx_in.1) | copy-start | bytes 3076
  0.7 0.7 %copy-start.1 = (s32[512]{0:T(512)S(1)}, s32[512]{0:T(512)}, u32[]{:S(2)}) copy-start(s32[512]{0:T(512)} %param.7) | copy-start | bytes 6148

commit v5 on v4

--- a/solution.py
+++ b/solution.py
@@ -9,6 +9,7 @@
 
 MESH = pl.DeviceIdType.MESH
 F32, BF16, I32 = jnp.float32, jnp.bfloat16, jnp.int32
+EARLY, PASSED_AFTER = (1, 2, 3), {3: 1, 0: 2, 4: 3}
 STATIONS, SLOTS, POLARS, CHANNELS, SPECTRA, ANTENNAS = 16, 16, 2, 16, 128, 256
 
 
@@ -40,8 +41,9 @@
     ]
     near_peer, far_peer = z_peer
     pair_peer = at((zh * 2 + 1 - par) * 4 + y, tile)
-    y_steps = [(e, d) for e in (0, 1) for d in (1, 3, 2)]
+    y_steps = [(e, d) for e in (0, 1) for d in (2, 1, 3)]
     y_peer = [at((zh * 2 + e) * 4 + (y + d) % 4, tile) for e, d in y_steps]
+    own_y_peer = [at(z * 4 + (y + d) % 4, tile) for d in (2, 1, 3)]
 
     barrier = pltpu.get_barrier_semaphore()
     partners = [sibling, *x_peer, pair_peer, *y_peer]
@@ -152,7 +154,7 @@
     for h in range(2):
         for p in range(POLARS):
             arrived(core_in.at[h, p], core_s.at[h, p], core_r.at[h, p])
-            for d in (1, 2, 3):
+            for d in (2, 1, 3):
                 to = (x + d) % 4
                 x_out[h, p, d - 1] = slabs[p, to, h, core] + core_in[h, p, to]
                 send(
@@ -160,6 +162,13 @@
                     x_s.at[h, p, d - 1], x_r.at[h, p, d - 1], x_peer[d - 1],
                 )
         lax.fori_loop(h * 16, h * 16 + 16, fill, 0)
+        if h == 1:
+
+            @pl.when(zi == 1)
+            def _():
+                for e in (2, 3):
+                    to_z(1, e).start()
+
         for p in range(POLARS):
             total = slabs[p, x, h, core] + core_in[h, p, x]
             for d in (1, 2, 3):
@@ -193,7 +202,7 @@
 
         @pl.when(zi != h)
         def _():
-            for e in range(4):
+            for e in range(2 if h == 0 else 4):
                 to_z(1, e).start()
 
     for d in (1, 2, 3, 0):
@@ -203,12 +212,28 @@
         held[source, 1 - par, y] = (near_in[source] + far_in[source].astype(F32)).astype(BF16)
         mine = held.at[source, 1 - par, y]
         send(mine, mine, y_s.at[d, 6], y_r.at[d, 1 - par, 0], pair_peer)
-        for j, (_, step) in enumerate(y_steps):
-            send(mine, mine, y_s.at[d, j], y_r.at[d, 1 - par, step], y_peer[j])
+        if d in EARLY:
+            for j, step in enumerate((2, 1, 3)):
+                send(mine, mine, y_s.at[d, j], y_r.at[d, 1 - par, step], own_y_peer[j])
+        else:
+            for j, (_, step) in enumerate(y_steps):
+                send(mine, mine, y_s.at[d, j], y_r.at[d, 1 - par, step], y_peer[j])
+        if d in PASSED_AFTER:
+            early = PASSED_AFTER[d]
+            other = held.at[(zh - early + 4) % 4, par, y]
+            arrived(other, y_s.at[early, 6], y_r.at[early, par, 0])
+            for j, step in enumerate((2, 1, 3)):
+                send(other, other, y_s.at[early, 3 + j], y_r.at[early, par, step], own_y_peer[j])
+    if 3 in EARLY:
+        other = held.at[(zh - 3 + 4) % 4, par, y]
+        arrived(other, y_s.at[3, 6], y_r.at[3, par, 0])
+        for j, step in enumerate((2, 1, 3)):
+            send(other, other, y_s.at[3, 3 + j], y_r.at[3, par, step], own_y_peer[j])
 
     for d in (1, 2, 3, 0):
         source = (zh - d + 4) % 4
-        arrived(held.at[source, par, y], y_s.at[d, 6], y_r.at[d, par, 0])
+        if d not in EARLY:
+            arrived(held.at[source, par, y], y_s.at[d, 6], y_r.at[d, par, 0])
         for j, (e, step) in enumerate(y_steps):
             arrived(held.at[source, 1 - e, (y - step + 4) % 4], y_s.at[d, j], y_r.at[d, 1 - e, step])
         right = jnp.concatenate(
@@ -250,7 +275,7 @@
     sem = pltpu.SemaphoreType.DMA
     out = pl.pallas_call(
         kernel,
-        out_shape=jax.ShapeDtypeStruct((2, 32, 1024), F32),
+        out_shape=pltpu.VMEM((2, 32, 1024), F32),
         in_specs=[hbm, hbm, hbm, hbm],
         out_specs=vmem,
         scratch_shapes=[
@@ -278,7 +303,7 @@
             sem((4, 7)), sem((4, 2, 4)),
         ],
         compiler_params=pltpu.CompilerParams(
-            collective_id=0, has_side_effects=True, vmem_limit_bytes=54700 * 1024
+            collective_id=0, has_side_effects=True, vmem_limit_bytes=56 * 2**20
         ),
     )(voltages, wt, antenna_slot_index, station_order.reshape(1, 512))
     return out[None]

time: 41 us -> 38.7 us (0.944)
  local copies, waits for them, and re-layouts: 2.08 us -> 0.71 us
  Pallas kernels: 38.7 us -> 37.5 us
    unnamed x5 -> x1, local copies, waits for them, and re-layouts: 2.08 us -> 0.71 us
    pallas_call x1, Pallas kernels: 38.7 us -> 37.5 us  [body(): pl.pallas_call(kernel, out_shape=pltpu.VMEM((2, 32, 1024), F32), in_specs...]
where the time goes in v5:
time: 38.7 us; the launch traced here: 38.2 us
  Pallas kernels  37.5 us (97%)
  local copies, waits for them, and re-layouts  0.71 us (2%)
    pallas_call x1, Pallas kernels, body(): pl.pallas_call(kernel, out_shape=pltpu.VMEM((2, 32, 1024), F32), in_specs...  37.5 us

profile of v5, /device:TPU:1, one launch (start us, length us, event | category | flops | bytes accessed | tf_op | source)
XLA Modules:
  0.0 38.2 jit_solution(14054829896710789232)
XLA Ops:
  0.0 37.5 %shard_map.46 = f32[2,32,1024]{2,1,0:T(8,128)S(1)} custom-call(bf16[2,16,16,2,16,128]{5,4,3,2,1,0:T(8,128)(2,1)} %volt.1, bf16[1024,256]{1,0:T(8,128)(2,1)} %bitcast.6, s32[16,16]{1,0:T(8,128)} %idx_in.1, s32[1,512]{1,0:T(1,128)} %bitcast.7), custom_call_target="tpu_custom_call" | custom-call | tf_op jit(solution)/shard_map/pallas_call | solution.py:276
  37.5 0.7 %copy.6 = f32[1,2,32,1024]{3,2,1,0:T(8,128)} copy(f32[1,2,32,1024]{3,2,1,0:T(8,128)S(1)} %bitcast.5) | data formatting | bytes 524288

commit v6 on v5

--- a/solution.py
+++ b/solution.py
@@ -23,8 +23,8 @@
 
 def kernel(
     volt, wt, idx_in, order_in, out,
-    idx, order, vbuf, wbuf, wexp, part, core_in, x_out, x_in, z_own, z_out, near_in, far_in, held, perm, summed, ordered,
-    i_sem, v_sem, w_sem, core_s, core_r, x_s, x_r, z_s, z_r, ready, y_s, y_r,
+    idx, order, vbuf, wbuf, wexp, part, x_wide, x_out, x_in, z_own, z_out, near_in, far_in, held, perm, summed, ordered,
+    i_sem, v_sem, w_sem, x_s, x_r, z_s, z_r, ready, y_s, y_r,
 ):
     group, tile = lax.axis_index("sgroup"), lax.axis_index("tile")
     z, y = group // 4, group % 4
@@ -34,8 +34,9 @@
     def at(g, t):
         return {"sgroup": g, "tile": t}
 
-    sibling = at(group, x * 4 + zi * 2 + (1 - core))
-    x_peer = [at(group, ((x + d) % 4) * 4 + zi * 2 + core) for d in (1, 2, 3)]
+    x_steps = [(0, 1), (1, 0), (3, 0), (2, 0), (2, 1), (1, 1), (3, 1)]
+    cores = (core, 1 - core)
+    x_peer = [at(group, ((x + d) % 4) * 4 + zi * 2 + cores[c]) for d, c in x_steps]
     z_peer = [
         [at((e * 2 + 1 - par) * 4 + y, x * 4 + half * 2 + core) for e in range(4)] for half in (zi, 1 - zi)
     ]
@@ -46,7 +47,7 @@
     own_y_peer = [at(z * 4 + (y + d) % 4, tile) for d in (2, 1, 3)]
 
     barrier = pltpu.get_barrier_semaphore()
-    partners = [sibling, *x_peer, pair_peer, *y_peer]
+    partners = [*x_peer, pair_peer, *y_peer]
 
     small = [
         pltpu.make_async_copy(idx_in, idx, i_sem.at[0]),
@@ -90,7 +91,7 @@
 
     def arrived(dst, s, r):
         pltpu.make_async_remote_copy(
-            src_ref=dst, dst_ref=dst, send_sem=s, recv_sem=r, device_id=sibling, device_id_type=MESH
+            src_ref=dst, dst_ref=dst, send_sem=s, recv_sem=r, device_id=pair_peer, device_id_type=MESH
         ).wait_recv()
 
     for copy in small:
@@ -125,6 +126,17 @@
             pl.semaphore_signal(ready, inc=1, device_id=partner, device_id_type=MESH)
 
     slabs = part.reshape(POLARS, 4, 2, 2, 2, STATIONS, SPECTRA)
+    def x_slot(h, p, j):
+        return x_wide.at[h, p, j] if j < 3 else x_in.at[h, p, j - 3]
+
+    def to_x(h, p):
+        for j, (d, c) in enumerate(x_steps):
+            source = slabs.at[p, (x + d) % 4, h, cores[c]]
+            if j >= 3:
+                x_out[h, p, j - 3] = source[...].astype(BF16)
+                source = x_out.at[h, p, j - 3]
+            send(source, x_slot(h, p, j), x_s.at[h, p, j], x_r.at[h, p, j], x_peer[j])
+
     for p in range(POLARS):
         for q in range(2):
             v_copies[p * 2 + q].wait()
@@ -140,9 +152,7 @@
                 imag = both[:16, SPECTRA:] + both[16:, :SPECTRA]
                 part[pl.ds(p * 512 + s, 16, stride=32), :] = real
                 part[pl.ds(p * 512 + 16 + s, 16, stride=32), :] = imag
-        for h in range(2):
-            theirs = slabs.at[p, :, h, 1 - core]
-            send(theirs, core_in.at[h, p], core_s.at[h, p], core_r.at[h, p], sibling)
+        to_x(0, p)
 
     def fill(step, carry):
         rows = (step % 8) * 128 + iota((128, 256), 0)
@@ -152,16 +162,10 @@
         return carry
 
     for h in range(2):
-        for p in range(POLARS):
-            arrived(core_in.at[h, p], core_s.at[h, p], core_r.at[h, p])
-            for d in (2, 1, 3):
-                to = (x + d) % 4
-                x_out[h, p, d - 1] = slabs[p, to, h, core] + core_in[h, p, to]
-                send(
-                    x_out.at[h, p, d - 1], x_in.at[h, p, d - 1],
-                    x_s.at[h, p, d - 1], x_r.at[h, p, d - 1], x_peer[d - 1],
-                )
-        lax.fori_loop(h * 16, h * 16 + 16, fill, 0)
+        if h == 0:
+            lax.fori_loop(0, 32, fill, 0)
+            for p in range(POLARS):
+                to_x(1, p)
         if h == 1:
 
             @pl.when(zi == 1)
@@ -170,10 +174,10 @@
                     to_z(1, e).start()
 
         for p in range(POLARS):
-            total = slabs[p, x, h, core] + core_in[h, p, x]
-            for d in (1, 2, 3):
-                arrived(x_in.at[h, p, d - 1], x_s.at[h, p, d - 1], x_r.at[h, p, d - 1])
-                total += x_in[h, p, d - 1]
+            total = slabs[p, x, h, core]
+            for j in range(7):
+                arrived(x_slot(h, p, j), x_s.at[h, p, j], x_r.at[h, p, j])
+                total += x_slot(h, p, j)[...].astype(F32)
 
             @pl.when(zi == h)
             def _():
@@ -230,7 +234,7 @@
         for j, step in enumerate((2, 1, 3)):
             send(other, other, y_s.at[3, 3 + j], y_r.at[3, par, step], own_y_peer[j])
 
-    for d in (1, 2, 3, 0):
+    for d in (1, 2, 0, 3):
         source = (zh - d + 4) % 4
         if d not in EARLY:
             arrived(held.at[source, par, y], y_s.at[d, 6], y_r.at[d, par, 0])
@@ -248,7 +252,7 @@
             got = jnp.dot(perm[source, rows, :], right, preferred_element_type=F32)
             if d == 1:
                 summed[rows, :] = got
-            elif d > 0:
+            elif d != 3:
                 summed[rows, :] += got
             else:
                 ordered[rows, :] = (summed[rows, :] + got).astype(BF16)
@@ -285,9 +289,9 @@
             pltpu.VMEM((1024, ANTENNAS), BF16),
             pltpu.VMEM((1024, 256), BF16),
             pltpu.VMEM((1024, SPECTRA), F32),
-            pltpu.VMEM((2, 2, 4, 2, STATIONS, SPECTRA), F32),
             pltpu.VMEM((2, 2, 3, 2, STATIONS, SPECTRA), F32),
-            pltpu.VMEM((2, 2, 3, 2, STATIONS, SPECTRA), F32),
+            pltpu.VMEM((2, 2, 4, 2, STATIONS, SPECTRA), BF16),
+            pltpu.VMEM((2, 2, 4, 2, STATIONS, SPECTRA), BF16),
             pltpu.VMEM((2, 2, STATIONS, SPECTRA), F32),
             pltpu.VMEM((2, 2, STATIONS, SPECTRA), BF16),
             pltpu.VMEM((4, 2, 2, STATIONS, SPECTRA), F32),
@@ -297,8 +301,7 @@
             pltpu.VMEM((1024, 256), F32),
             pltpu.VMEM((1024, 256), BF16),
             sem((2,)), sem((2, 2)), sem,
-            sem((2, 2)), sem((2, 2)),
-            sem((2, 2, 3)), sem((2, 2, 3)),
+            sem((2, 2, 7)), sem((2, 2, 7)),
             sem((2, 4)), sem((2, 4)), pltpu.SemaphoreType.REGULAR,
             sem((4, 7)), sem((4, 2, 4)),
         ],

time: 38.7 us -> 37.9 us (0.979)
  Pallas kernels: 37.5 us -> 37 us
    pallas_call x1, Pallas kernels: 37.5 us -> 37 us  [body(): pl.pallas_call(kernel, out_shape=pltpu.VMEM((2, 32, 1024), F32), in_specs...]
where the time goes in v6:
time: 37.9 us; the launch traced here: 37.8 us
  Pallas kernels  37 us (98%)
  local copies, waits for them, and re-layouts  0.71 us (2%)
    pallas_call x1, Pallas kernels, body(): pl.pallas_call(kernel, out_shape=pltpu.VMEM((2, 32, 1024), F32), in_specs...  37 us

profile of v6, /device:TPU:1, one launch (start us, length us, event | category | flops | bytes accessed | tf_op | source)
XLA Modules:
  0.0 37.8 jit_solution(9263280013857461315)
XLA Ops:
  0.0 37.0 %shard_map.46 = f32[2,32,1024]{2,1,0:T(8,128)S(1)} custom-call(bf16[2,16,16,2,16,128]{5,4,3,2,1,0:T(8,128)(2,1)} %volt.1, bf16[1024,256]{1,0:T(8,128)(2,1)} %bitcast.6, s32[16,16]{1,0:T(8,128)} %idx_in.1, s32[1,512]{1,0:T(1,128)} %bitcast.7), custom_call_target="tpu_custom_call" | custom-call | tf_op jit(solution)/shard_map/pallas_call | solution.py:280
  37.0 0.7 %copy.6 = f32[1,2,32,1024]{3,2,1,0:T(8,128)} copy(f32[1,2,32,1024]{3,2,1,0:T(8,128)S(1)} %bitcast.5) | data formatting | bytes 524288

commit v7 on v6

--- a/solution.py
+++ b/solution.py
@@ -59,12 +59,9 @@
     w_copy.start()
     v_copies = []
     for p in range(POLARS):
-        for q in range(2):
-            copy = pltpu.make_async_copy(
-                volt.at[:, pl.ds(q * 8, 8), :, p], vbuf.at[p, :, pl.ds(q * 8, 8)], v_sem.at[p, q]
-            )
-            copy.start()
-            v_copies.append(copy)
+        copy = pltpu.make_async_copy(volt.at[:, :, :, p], vbuf.at[p], v_sem.at[p])
+        copy.start()
+        v_copies.append(copy)
 
     for partner in partners:
         pl.semaphore_signal(barrier, inc=1, device_id=partner, device_id_type=MESH)
@@ -138,20 +135,19 @@
             send(source, x_slot(h, p, j), x_s.at[h, p, j], x_r.at[h, p, j], x_peer[j])
 
     for p in range(POLARS):
-        for q in range(2):
-            v_copies[p * 2 + q].wait()
-            for s in range(q * 8, q * 8 + 8):
-                left = jnp.concatenate(
-                    [wexp[pl.ds(((k * STATIONS + s) * 2 + p) * 16, 16), :] for k in (0, 1)], axis=0
-                )
-                right = jnp.concatenate(
-                    [vbuf[p, k, s].reshape(lanes, SPECTRA) for k in (0, 1)], axis=1
-                )
-                both = jnp.dot(left, right, preferred_element_type=F32)
-                real = both[:16, :SPECTRA] - both[16:, SPECTRA:]
-                imag = both[:16, SPECTRA:] + both[16:, :SPECTRA]
-                part[pl.ds(p * 512 + s, 16, stride=32), :] = real
-                part[pl.ds(p * 512 + 16 + s, 16, stride=32), :] = imag
+        v_copies[p].wait()
+        for s in range(STATIONS):
+            left = jnp.concatenate(
+                [wexp[pl.ds(((k * STATIONS + s) * 2 + p) * 16, 16), :] for k in (0, 1)], axis=0
+            )
+            right = jnp.concatenate(
+                [vbuf[p, k, s].reshape(lanes, SPECTRA) for k in (0, 1)], axis=1
+            )
+            both = jnp.dot(left, right, preferred_element_type=F32)
+            real = both[:16, :SPECTRA] - both[16:, SPECTRA:]
+            imag = both[:16, SPECTRA:] + both[16:, :SPECTRA]
+            part[pl.ds(p * 512 + s, 16, stride=32), :] = real
+            part[pl.ds(p * 512 + 16 + s, 16, stride=32), :] = imag
         to_x(0, p)
 
     def fill(step, carry):
@@ -300,7 +296,7 @@
             pltpu.VMEM((4, 1024, 256), BF16),
             pltpu.VMEM((1024, 256), F32),
             pltpu.VMEM((1024, 256), BF16),
-            sem((2,)), sem((2, 2)), sem,
+            sem((2,)), sem((2,)), sem,
             sem((2, 2, 7)), sem((2, 2, 7)),
             sem((2, 4)), sem((2, 4)), pltpu.SemaphoreType.REGULAR,
             sem((4, 7)), sem((4, 2, 4)),

time: 37.9 us -> 37.5 us (0.989)
  no operation moved by 1% of the time
where the time goes in v7:
time: 37.5 us; the launch traced here: 37.4 us
  Pallas kernels  36.7 us (98%)
  local copies, waits for them, and re-layouts  0.71 us (2%)
    pallas_call x1, Pallas kernels, body(): pl.pallas_call(kernel, out_shape=pltpu.VMEM((2, 32, 1024), F32), in_specs...  36.7 us

profile of v7, /device:TPU:1, one launch (start us, length us, event | category | flops | bytes accessed | tf_op | source)
XLA Modules:
  0.0 37.4 jit_solution(5715984131099293919)
XLA Ops:
  0.0 36.7 %shard_map.46 = f32[2,32,1024]{2,1,0:T(8,128)S(1)} custom-call(bf16[2,16,16,2,16,128]{5,4,3,2,1,0:T(8,128)(2,1)} %volt.1, bf16[1024,256]{1,0:T(8,128)(2,1)} %bitcast.6, s32[16,16]{1,0:T(8,128)} %idx_in.1, s32[1,512]{1,0:T(1,128)} %bitcast.7), custom_call_target="tpu_custom_call" | custom-call | tf_op jit(solution)/shard_map/pallas_call | solution.py:276
  36.7 0.7 %copy.6 = f32[1,2,32,1024]{3,2,1,0:T(8,128)} copy(f32[1,2,32,1024]{3,2,1,0:T(8,128)S(1)} %bitcast.5) | data formatting | bytes 524288
